TPU v7x, 32 devices: a whole 2x2x4 slice. The times are simulated.
32 devices in a mesh: grp: 8 (over y, x, core), sub: 4 (over z).
Axes of the slice: x: 2, y: 2, z: 4, core: 2. Of those that a mesh axis runs over, the one named last changes fastest.
Arguments:
- ratings: bfloat16 [32768, 4, 256], P(('grp', 'sub')), may hold values from -6 to 6
- present: int32 [256, 4, 2], P(('grp', 'sub')), may hold values from 0 to 1, as said below
- user_factors: float32 [32768, 256], P(('grp', 'sub')), may hold values from -1.5 to 1.5
- item_factors: float32 [2048, 256], P(('grp', 'sub')), may hold values from -1.5 to 1.5
Outputs:
- users_out: float32 [32768, 256], P(('grp', 'sub'))
- items_out: float32 [2048, 256], P(('grp', 'sub'))
Inputs may be any that keep to these rules, and one draw needn't show every extreme that they name: 1 marks a present tile of 128 users by 128 items, 0 an absent one; the share of present tiles differs from device to device.
All inputs are finite; a program needn't handle non-finite values.
Results may differ from a plain program's by a relative error of at most 0.0003.
Values sent between devices are 32-bit elements; how exact they have to be, the bound alone decides.
A program may use at most 64 MiB of HBM per device.

v0:
```python
import jax
import jax.numpy as jnp
from jax import lax
from jax.sharding import PartitionSpec as P

TILE = 128
TICKS = 4


user_rate = 0.05
item_rate = 0.0008
shrink_rate = 0.05


def passed_along(value, axis, steps):
    count = lax.axis_size(axis)
    pairs = [(source, (source + steps) % count) for source in range(count)]
    return lax.ppermute(value, axis, pairs)


def expand_mask(marks, tile_size):
    tall, wide = marks.shape
    filled = jnp.broadcast_to(
        marks[:, None, :, None].astype(jnp.float32), (tall, tile_size, wide, tile_size)
    )
    return filled.reshape(tall * tile_size, wide * tile_size)


def local_errors(user_rows, rating_now, marks_now, item_block):
    filled = expand_mask(marks_now, TILE)
    predicted = jnp.dot(
        user_rows, item_block.T, precision=lax.Precision.HIGHEST, preferred_element_type=jnp.float32
    )
    errors = filled * (rating_now.astype(jnp.float32) - predicted)
    user_grad = (
        jnp.dot(
            errors, item_block, precision=lax.Precision.HIGHEST, preferred_element_type=jnp.float32
        )
        - shrink_rate * user_rows
    )
    return (errors, user_rows + user_rate * user_grad)


def on_device(ratings, present, user_factors, item_factors):
    user_rows = user_factors
    shard_rows = item_factors.shape[0]
    item_shard = item_factors
    for tick_index in range(TICKS):
        item_block = lax.all_gather(item_shard, "sub", axis=0, tiled=True)
        errors, user_next = local_errors(
            user_rows, ratings[:, tick_index, :], present[:, tick_index, :], item_block
        )
        current_users = user_rows

        def item_term(row_start, row_count, errors=errors, current_users=current_users):
            return jnp.dot(
                errors.T,
                current_users,
                precision=lax.Precision.HIGHEST,
                preferred_element_type=jnp.float32,
            )

        summed = lax.psum_scatter(
            item_term(jnp.int32(0), lax.axis_size("sub") * shard_rows),
            "sub",
            scatter_dimension=0,
            tiled=True,
        )
        item_shard = item_shard + item_rate * (summed - shrink_rate * item_shard)
        user_rows = user_next
        item_shard = passed_along(item_shard, "grp", 1)
    return (user_rows, item_shard)


def solution(mesh):
    in_specs = (
        P(("grp", "sub"), None, None),
        P(("grp", "sub"), None, None),
        P(("grp", "sub"), None),
        P(("grp", "sub"), None),
    )
    out_specs = (P(("grp", "sub"), None), P(("grp", "sub"), None))
    return jax.shard_map(
        on_device, mesh=mesh, in_specs=in_specs, out_specs=out_specs, check_vma=False
    )
```

profile of v0, /device:TPU:0, one launch (start us, length us, event | category | flops | bytes accessed | tf_op | source)
XLA Modules:
  0.0 193.4 jit_solution(18212341932760408945)
XLA Ops:
  7.2 8.9 %fusion.12 = (bf16[1024,1,256]{2,1,0:T(2,128)(2,1)}, bf16[1024,1,256]{2,1,0:T(2,128)(2,1)}, bf16[1024,1,256]{2,1,0:T(2,128)(2,1)}, bf16[1024,1,256]{2,1,0:T(2,128)(2,1)S(1)}) fusion(bf16[1024,4,256]{2,1,0:T(4,128)(2,1)} %param.4), kind=kLoop, calls=%fused_computation.32 | loop fusion | bytes 4194304 | tf_op jit(solution)/shard_map/slice | solution.py:51
  16.2 15.7 %all_gather.12 = f32[256,256]{1,0:T(8,128)S(1)} all-gather(f32[64,256]{1,0:T(8,128)S(1)} %copy-done.3), channel_id=1, replica_groups=mesh['grp'=8,'sub'=4] {'sub'}, dimensions={0}, use_global_device_ids=true | all-gather | bytes 327680 | tf_op jit(solution)/shard_map/all_gather | solution.py:49
  32.3 1.0 fusion.11
  33.4 2.5 %fusion.13 = f32[256,256]{1,0:T(8,128)} fusion(f32[1024,256]{1,0:T(8,128)S(1)} %fusion.11, f32[1024,256]{1,0:T(8,128)S(1)} %copy-done), kind=kOutput, calls=%fused_computation.33 | convolution fusion | flops 805306368 | bytes 2359296 | tf_op jit(solution)/shard_map/dot_general | solution.py:56
  35.9 21.3 %reduce-scatter.5.cloned.1.call-done = f32[64,256]{1,0:T(8,128)} async-done(((f32[256,256]{1,0:T(8,128)}), f32[64,256]{1,0:T(8,128)}) %reduce-scatter.5.cloned.1.call-update) | async-done | bytes 65552 | tf_op jit(solution)/shard_map/reduce_scatter | solution.py:63
  57.2 0.9 multiply_add_fusion.3
  58.2 1.0 fusion.10
  59.2 3.5 %collective-permute-done = f32[64,256]{1,0:T(8,128)S(1)} collective-permute-done((f32[64,256]{1,0:T(8,128)S(1)}, f32[64,256]{1,0:T(8,128)S(1)}, u32[]{:S(2)}, u32[]{:S(2)}) %collective-permute-start) | collective-permute-done | bytes 65568 | tf_op jit(solution)/shard_map/ppermute | solution.py:18
  62.7 13.8 %all_gather.13 = f32[256,256]{1,0:T(8,128)S(1)} all-gather(f32[64,256]{1,0:T(8,128)S(1)} %collective-permute-done), channel_id=1, replica_groups=mesh['grp'=8,'sub'=4] {'sub'}, dimensions={0}, use_global_device_ids=true | all-gather | bytes 327680 | tf_op jit(solution)/shard_map/all_gather | solution.py:49
  76.9 2.2 %fusion.8 = f32[1024,256]{1,0:T(8,128)S(1)} fusion(f32[1024,256]{1,0:T(8,128)S(1)} %fusion.10, f32[256,256]{1,0:T(8,128)S(1)} %all_gather.13, f32[128,8,2,128]{3,2,1,0:T(2,128)S(1)} %bitcast.69, bf16[1024,1,256]{2,1,0:T(2,128)(2,1)} %get-tuple-element.4), kind=kOutput, calls=%fused_computation.14 | convolution fusion | flops 806092800 | bytes 3932160 | tf_op jit(solution)/shard_map/dot_general | solution.py:31
  79.2 2.5 %fusion.14 = f32[256,256]{1,0:T(8,128)} fusion(f32[1024,256]{1,0:T(8,128)S(1)} %fusion.8, f32[1024,256]{1,0:T(8,128)S(1)} %fusion.10), kind=kOutput, calls=%fused_computation.34 | convolution fusion | flops 805306368 | bytes 2359296 | tf_op jit(solution)/shard_map/dot_general | solution.py:56
  81.9 17.2 %reduce-scatter.7.cloned.1.call-done = f32[64,256]{1,0:T(8,128)} async-done(((f32[256,256]{1,0:T(8,128)}), f32[64,256]{1,0:T(8,128)}) %reduce-scatter.7.cloned.1.call-update) | async-done | bytes 65552 | tf_op jit(solution)/shard_map/reduce_scatter | solution.py:63
  99.0 0.9 multiply_add_fusion.2
  100.0 1.0 fusion.7
  101.0 3.6 %collective-permute-done.1 = f32[64,256]{1,0:T(8,128)S(1)} collective-permute-done((f32[64,256]{1,0:T(8,128)S(1)}, f32[64,256]{1,0:T(8,128)S(1)}, u32[]{:S(2)}, u32[]{:S(2)}) %collective-permute-start.1) | collective-permute-done | bytes 65568 | tf_op jit(solution)/shard_map/ppermute | solution.py:18
  104.6 14.0 %all_gather.14 = f32[256,256]{1,0:T(8,128)S(1)} all-gather(f32[64,256]{1,0:T(8,128)S(1)} %collective-permute-done.1), channel_id=1, replica_groups=mesh['grp'=8,'sub'=4] {'sub'}, dimensions={0}, use_global_device_ids=true | all-gather | bytes 327680 | tf_op jit(solution)/shard_map/all_gather | solution.py:49
  118.6 0.3 broadcast_in_dim.10
  118.9 1.0 fusion.5
  120.0 2.5 %fusion.15 = f32[256,256]{1,0:T(8,128)} fusion(f32[1024,256]{1,0:T(8,128)S(1)} %fusion.5, f32[1024,256]{1,0:T(8,128)S(1)} %fusion.7), kind=kOutput, calls=%fused_computation.35 | convolution fusion | flops 805306368 | bytes 2359296 | tf_op jit(solution)/shard_map/dot_general | solution.py:56
  122.7 17.3 %reduce-scatter.9.cloned.1.call-done = f32[64,256]{1,0:T(8,128)} async-done(((f32[256,256]{1,0:T(8,128)}), f32[64,256]{1,0:T(8,128)}) %reduce-scatter.9.cloned.1.call-update) | async-done | bytes 65552 | tf_op jit(solution)/shard_map/reduce_scatter | solution.py:63
  139.9 0.9 multiply_add_fusion.1
  140.9 1.0 fusion.4
  141.8 3.6 %collective-permute-done.2 = f32[64,256]{1,0:T(8,128)S(1)} collective-permute-done((f32[64,256]{1,0:T(8,128)S(1)}, f32[64,256]{1,0:T(8,128)S(1)}, u32[]{:S(2)}, u32[]{:S(2)}) %collective-permute-start.2) | collective-permute-done | bytes 65568 | tf_op jit(solution)/shard_map/ppermute | solution.py:18
  145.4 13.9 %all_gather.15 = f32[256,256]{1,0:T(8,128)S(1)} all-gather(f32[64,256]{1,0:T(8,128)S(1)} %collective-permute-done.2), channel_id=1, replica_groups=mesh['grp'=8,'sub'=4] {'sub'}, dimensions={0}, use_global_device_ids=true | all-gather | bytes 327680 | tf_op jit(solution)/shard_map/all_gather | solution.py:49
  159.3 0.3 broadcast_in_dim.11
  159.7 1.0 fusion.2
  160.7 2.5 %fusion.16 = f32[256,256]{1,0:T(8,128)} fusion(f32[1024,256]{1,0:T(8,128)S(1)} %fusion.2, f32[1024,256]{1,0:T(8,128)S(1)} %fusion.4), kind=kOutput, calls=%fused_computation.36 | convolution fusion | flops 805306368 | bytes 2359296 | tf_op jit(solution)/shard_map/dot_general | solution.py:56
  163.2 17.5 %reduce-scatter.11.cloned.1.call-done = f32[64,256]{1,0:T(8,128)} async-done(((f32[256,256]{1,0:T(8,128)}), f32[64,256]{1,0:T(8,128)}) %reduce-scatter.11.cloned.1.call-update) | async-done | bytes 65552 | tf_op jit(solution)/shard_map/reduce_scatter | solution.py:63
  180.7 0.9 multiply_add_fusion
  181.7 2.0 %fusion.1 = f32[1024,256]{1,0:T(8,128)} fusion(f32[1024,256]{1,0:T(8,128)S(1)} %fusion.4, f32[1024,256]{1,0:T(8,128)S(1)} %fusion.2, f32[256,256]{1,0:T(8,128)S(1)} %all_gather.15), kind=kOutput, calls=%fused_computation.2 | convolution fusion | flops 806354944 | bytes 3407872 | tf_op jit(solution)/shard_map/dot_general | solution.py:36
  183.6 2.6 %collective-permute-done.3 = f32[64,256]{1,0:T(8,128)S(1)} collective-permute-done((f32[64,256]{1,0:T(8,128)S(1)}, f32[64,256]{1,0:T(8,128)S(1)}, u32[]{:S(2)}, u32[]{:S(2)}) %collective-permute-start.3) | collective-permute-done | bytes 65568 | tf_op jit(solution)/shard_map/ppermute | solution.py:18
  186.2 0.6 copy.39
  (29 shorter events, 1.5 us)
Async XLA Ops:
  7.2 8.9 %copy-start.4 = (s32[8,4,2]{0,2,1:T(2,128)S(1)}, s32[8,4,2]{0,2,1:T(2,128)}, u32[]{:S(2)}) copy-start(s32[8,4,2]{0,2,1:T(2,128)} %param.5) | copy-start | bytes 772
  7.2 9.0 %copy-start.3 = (f32[64,256]{1,0:T(8,128)S(1)}, f32[64,256]{1,0:T(8,128)}, u32[]{:S(2)}) copy-start(f32[64,256]{1,0:T(8,128)} %param.7) | copy-start | bytes 196612
  7.2 50.1 %reduce-scatter.5.cloned.1.call-start = ((), (), s32[]{:S(2)}) async-start(), calls=%async_computation.4 | async-start | bytes 327680 | tf_op jit(solution)/shard_map/reduce_scatter | solution.py:63
  16.1 16.2 %copy-start = (f32[1024,256]{1,0:T(8,128)S(1)}, f32[1024,256]{1,0:T(8,128)}, u32[]{:S(2)}) copy-start(f32[1024,256]{1,0:T(8,128)} %param.6) | copy-start | bytes 3145732
  35.9 63.1 %reduce-scatter.7.cloned.1.call-start = ((), (), s32[]{:S(2)}) async-start(), calls=%async_computation.5 | async-start | bytes 327680 | tf_op jit(solution)/shard_map/reduce_scatter | solution.py:63
  58.1 4.6 %collective-permute-start = (f32[64,256]{1,0:T(8,128)S(1)}, f32[64,256]{1,0:T(8,128)S(1)}, u32[]{:S(2)}, u32[]{:S(2)}) collective-permute-start(f32[64,256]{1,0:T(8,128)S(1)} %multiply_add_fusion.3), channel_id=1, source_target_pairs={{0,4},{4,8},{8,12},{12,16},{16,20},{20,24},{24,28},{28,0},{1,5},{5... | collective-permute-start | bytes 196616 | tf_op jit(solution)/shard_map/ppermute | solution.py:18
  81.7 58.2 %reduce-scatter.9.cloned.1.call-start = ((), (), s32[]{:S(2)}) async-start(), calls=%async_computation.6 | async-start | bytes 327680 | tf_op jit(solution)/shard_map/reduce_scatter | solution.py:63
  99.9 19.0 %copy-start.2 = (bf16[1024,1,256]{2,1,0:T(2,128)(2,1)S(1)}, bf16[1024,1,256]{2,1,0:T(2,128)(2,1)}, u32[]{:S(2)}) copy-start(bf16[1024,1,256]{2,1,0:T(2,128)(2,1)} %get-tuple-element.3) | copy-start | bytes 1572868
  99.9 4.6 %collective-permute-start.1 = (f32[64,256]{1,0:T(8,128)S(1)}, f32[64,256]{1,0:T(8,128)S(1)}, u32[]{:S(2)}, u32[]{:S(2)}) collective-permute-start(f32[64,256]{1,0:T(8,128)S(1)} %multiply_add_fusion.2), channel_id=1, source_target_pairs={{0,4},{4,8},{8,12},{12,16},{16,20},{20,24},{24,28},{28,0},{1,5},{5... | collective-permute-start | bytes 196616 | tf_op jit(solution)/shard_map/ppermute | solution.py:18
  122.5 58.2 %reduce-scatter.11.cloned.1.call-start = ((), (), s32[]{:S(2)}) async-start(), calls=%async_computation.7 | async-start | bytes 327680 | tf_op jit(solution)/shard_map/reduce_scatter | solution.py:63
  140.8 18.9 %copy-start.1 = (bf16[1024,1,256]{2,1,0:T(2,128)(2,1)S(1)}, bf16[1024,1,256]{2,1,0:T(2,128)(2,1)}, u32[]{:S(2)}) copy-start(bf16[1024,1,256]{2,1,0:T(2,128)(2,1)} %get-tuple-element.2) | copy-start | bytes 1572868
  140.8 4.6 %collective-permute-start.2 = (f32[64,256]{1,0:T(8,128)S(1)}, f32[64,256]{1,0:T(8,128)S(1)}, u32[]{:S(2)}, u32[]{:S(2)}) collective-permute-start(f32[64,256]{1,0:T(8,128)S(1)} %multiply_add_fusion.1), channel_id=1, source_target_pairs={{0,4},{4,8},{8,12},{12,16},{16,20},{20,24},{24,28},{28,0},{1,5},{5... | collective-permute-start | bytes 196616 | tf_op jit(solution)/shard_map/ppermute | solution.py:18
  181.6 4.6 %collective-permute-start.3 = (f32[64,256]{1,0:T(8,128)S(1)}, f32[64,256]{1,0:T(8,128)S(1)}, u32[]{:S(2)}, u32[]{:S(2)}) collective-permute-start(f32[64,256]{1,0:T(8,128)S(1)} %multiply_add_fusion), channel_id=1, source_target_pairs={{0,4},{4,8},{8,12},{12,16},{16,20},{20,24},{24,28},{28,0},{1,5},{5... | collective-permute-start | bytes 196616 | tf_op jit(solution)/shard_map/ppermute | solution.py:18
Sparse Core Ops, SparseCore 0:
  36.0 21.1 reduce-scatter.4
  81.8 17.1 reduce-scatter.6
  122.6 17.2 reduce-scatter.8
  163.4 17.3 reduce-scatter.10
where the time goes:
time: 194 us; the launch traced here: 193 us
  waiting for transfers between devices  86.6 us (45%)
  blocking collectives  57.5 us (30%)
  matrix products  20.4 us (11%)
  between operations  14 us (7%)
  local copies, waits for them, and re-layouts  11.2 us (6%)
  other arithmetic  3.42 us (2%)
    reduce_scatter x4, waiting for transfers between devices, on_device(): lax.psum_scatter(item_term(jnp.int32(0), lax.axis_size('sub') * shard_row...  73.2 us
    all_gather x4, blocking collectives, on_device(): item_block = lax.all_gather(item_shard, 'sub', axis=0, tiled=True)  57.5 us
    ppermute x4, waiting for transfers between devices, passed_along(): return lax.ppermute(value, axis, pairs)  13.3 us
    dot_general x4, matrix products, item_term(): jnp.dot(errors.T, current_users, precision=lax.Precision.HIGHEST, preferr...  10.1 us
    slice x1, local copies, waits for them, and re-layouts, on_device(): ratings[:, tick_index, :]  8.88 us
    dot_general x4, matrix products, local_errors(): jnp.dot(user_rows, item_block.T, precision=lax.Precision.HIGHEST, preferr...  5.33 us
    dot_general x4, matrix products, local_errors(): jnp.dot(errors, item_block, precision=lax.Precision.HIGHEST, preferred_el...  4.93 us
  transfers between devices with their start and end apart: 8, of which 8 were waited for; matrix products, arithmetic and copies ran while one was open for 3% of the time, Pallas kernels for 0%

commit v1 on v0

v1 whole, which is shorter than its diff:
```python
import functools

import jax
import jax.numpy as jnp
from jax import lax
from jax.experimental import pallas as pl
from jax.experimental.pallas import tpu as pltpu
from jax.sharding import PartitionSpec as P

TILE = 128

user_rate = 0.05
item_rate = 0.0008
shrink_rate = 0.05

MESH = pl.DeviceIdType.MESH
NT = ((1,), (1,))
NN = ((1,), (0,))
TN = ((0,), (0,))


def mm(left, right, dims):
    return lax.dot_general(left, right, (dims, ((), ())), preferred_element_type=jnp.float32)


def split(value):
    high = value.astype(jnp.bfloat16)
    low = (value - high.astype(jnp.float32)).astype(jnp.bfloat16)
    return high, low


def kernel(
    n_grp, n_sub, ticks, parts,
    marks, ratings, users, items, users_out, items_out,
    uh, ul, eh, el, vbuf, gbuf, rbuf, stage, vfin,
    init_send, init_recv, rs_send, rs_recv, ag_send, ag_recv, fin_send, fin_recv,
):
    grp = lax.axis_index("grp")
    sub = lax.axis_index("sub")
    after = lax.rem(grp + 1, n_grp)
    before = lax.rem(grp + n_grp - 1, n_grp)
    shard = items.shape[0]
    piece = TILE // n_sub
    user_tiles = users.shape[0] // TILE

    barrier = pltpu.get_barrier_semaphore()
    for k in range(1, n_sub):
        pl.semaphore_signal(barrier, inc=1, device_id=(grp, lax.rem(sub + k, n_sub)), device_id_type=MESH)
    for k in range(n_sub):
        pl.semaphore_signal(barrier, inc=1, device_id=(before, lax.rem(sub + k, n_sub)), device_id_type=MESH)
    pl.semaphore_wait(barrier, 2 * n_sub - 1)

    def init_copy(k):
        peer = lax.rem(sub + k, n_sub)
        return pltpu.make_async_remote_copy(
            src_ref=items,
            dst_ref=vbuf.at[0, pl.ds(sub * shard, shard), :],
            send_sem=init_send.at[k], recv_sem=init_recv.at[k],
            device_id=(grp, peer), device_id_type=MESH,
        )

    for k in range(1, n_sub):
        init_copy(k).start()
    vbuf[0, pl.ds(sub * shard, shard), :] = items[...]
    high, low = split(users[...])
    uh[...] = high
    ul[...] = low
    users_out[...] = users[...]
    for k in range(1, n_sub):
        init_copy(k).wait()

    def rs_copy(t, p, k):
        peer = lax.rem(sub + k, n_sub)
        return pltpu.make_async_remote_copy(
            src_ref=gbuf.at[p, pl.ds(peer * piece, piece), :],
            dst_ref=rbuf.at[t, p, k],
            send_sem=rs_send.at[p, k], recv_sem=rs_recv.at[t, p, k],
            device_id=(grp, peer), device_id_type=MESH,
        )

    def ag_copy(t, p, k):
        peer = lax.rem(sub + k, n_sub)
        return pltpu.make_async_remote_copy(
            src_ref=stage.at[p],
            dst_ref=vbuf.at[t + 1, pl.ds(p * TILE + sub * piece, piece), :],
            send_sem=ag_send.at[p, k], recv_sem=ag_recv.at[t, p, k],
            device_id=(after, peer), device_id_type=MESH,
        )

    def fin_copy(p):
        row = p * TILE + sub * piece
        return pltpu.make_async_remote_copy(
            src_ref=stage.at[p],
            dst_ref=vfin.at[pl.ds(lax.rem(row, shard), piece), :],
            send_sem=fin_send.at[p], recv_sem=fin_recv.at[lax.rem(row, shard) // piece],
            device_id=(after, row // shard), device_id_type=MESH,
        )

    def tick(t, carry):
        for p in range(parts):
            cols = slice(p * TILE, (p + 1) * TILE)

            @pl.when(t > 0)
            def _():
                for k in range(n_sub):
                    ag_copy(t - 1, p, k).wait_recv()

            vh, vl = split(vbuf[t, cols, :])
            pred = mm(uh[...], vh, NT) + mm(uh[...], vl, NT) + mm(ul[...], vh, NT)
            for i in range(user_tiles):
                rows = slice(i * TILE, (i + 1) * TILE)
                mark = marks[(i * ticks + t) * parts + p].astype(jnp.float32)
                error = mark * (ratings[t, rows, cols].astype(jnp.float32) - pred[rows, :])
                high, low = split(error)
                eh[rows, cols] = high
                el[rows, cols] = low
            gbuf[p] = (
                mm(eh[:, cols], uh[...], TN) + mm(eh[:, cols], ul[...], TN) + mm(el[:, cols], uh[...], TN)
            )
            for k in range(1, n_sub):
                rs_copy(t, p, k).start()

        vh, vl = split(vbuf[t])
        grad = mm(eh[...], vh, NN) + mm(eh[...], vl, NN) + mm(el[...], vh, NN)
        old = users_out[...]
        new = old + user_rate * (grad - shrink_rate * old)
        users_out[...] = new
        high, low = split(new)
        uh[...] = high
        ul[...] = low

        for p in range(parts):
            total = gbuf[p, pl.ds(sub * piece, piece), :]
            for k in range(1, n_sub):
                rs_copy(t, p, k).wait_recv()
                total = total + rbuf[t, p, k]
            mine = vbuf[t, pl.ds(p * TILE + sub * piece, piece), :]
            stage[p] = mine + item_rate * (total - shrink_rate * mine)

            @pl.when(t < ticks - 1)
            def _():
                for k in range(n_sub):
                    ag_copy(t, p, k).start()

            @pl.when(t == ticks - 1)
            def _():
                fin_copy(p).start()

        for p in range(parts):
            for k in range(1, n_sub):
                rs_copy(t, p, k).wait_send()

            @pl.when(t < ticks - 1)
            def _():
                for k in range(n_sub):
                    ag_copy(t, p, k).wait_send()

        return carry

    lax.fori_loop(0, ticks, tick, 0)
    for p in range(parts):
        fin_copy(p).wait_send()
    for p in range(parts):
        pltpu.make_async_remote_copy(
            src_ref=stage.at[p], dst_ref=vfin.at[pl.ds(p * piece, piece), :],
            send_sem=fin_send.at[p], recv_sem=fin_recv.at[p],
            device_id=(after, sub), device_id_type=MESH,
        ).wait_recv()
    items_out[...] = vfin[...]


def on_device(n_grp, n_sub, ratings, present, user_factors, item_factors):
    n_users, ticks, block = ratings.shape
    rank = user_factors.shape[1]
    parts = block // TILE
    piece = TILE // n_sub
    shard = item_factors.shape[0]
    f32, bf16 = jnp.float32, jnp.bfloat16
    dma = pltpu.SemaphoreType.DMA
    vmem = pl.BlockSpec(memory_space=pltpu.VMEM)
    return pl.pallas_call(
        functools.partial(kernel, n_grp, n_sub, ticks, parts),
        out_shape=(
            jax.ShapeDtypeStruct(user_factors.shape, f32),
            jax.ShapeDtypeStruct(item_factors.shape, f32),
        ),
        in_specs=[pl.BlockSpec(memory_space=pltpu.SMEM), vmem, vmem, vmem],
        out_specs=(vmem, vmem),
        scratch_shapes=[
            pltpu.VMEM((n_users, rank), bf16),
            pltpu.VMEM((n_users, rank), bf16),
            pltpu.VMEM((n_users, block), bf16),
            pltpu.VMEM((n_users, block), bf16),
            pltpu.VMEM((ticks, block, rank), f32),
            pltpu.VMEM((parts, TILE, rank), f32),
            pltpu.VMEM((ticks, parts, n_sub, piece, rank), f32),
            pltpu.VMEM((parts, piece, rank), f32),
            pltpu.VMEM((shard, rank), f32),
            dma((n_sub,)), dma((n_sub,)),
            dma((parts, n_sub)), dma((ticks, parts, n_sub)),
            dma((parts, n_sub)), dma((ticks, parts, n_sub)),
            dma((parts,)), dma((parts,)),
        ],
        compiler_params=pltpu.CompilerParams(
            collective_id=0, has_side_effects=True, vmem_limit_bytes=48 * 1024 * 1024
        ),
    )(present.reshape(-1), jnp.transpose(ratings, (1, 0, 2)), user_factors, item_factors)


def solution(mesh):
    both = ("grp", "sub")
    return jax.shard_map(
        functools.partial(on_device, mesh.shape["grp"], mesh.shape["sub"]),
        mesh=mesh,
        in_specs=(P(both, None, None), P(both, None, None), P(both, None), P(both, None)),
        out_specs=(P(both, None), P(both, None)),
        check_vma=False,
    )
```

time: 194 us -> 68.1 us (0.35)
  waiting for transfers between devices: 86.6 us -> 0 us
  Pallas kernels: 0 us -> 62.8 us
  blocking collectives: 57.5 us -> 0 us
  matrix products: 20.4 us -> 0 us
  between operations: 14 us -> 0.68 us
  local copies, waits for them, and re-layouts: 11.2 us -> 4.46 us
  other arithmetic: 3.42 us -> 0 us
    reduce_scatter x4 -> x0, waiting for transfers between devices: 73.2 us -> none  [on_device(): lax.psum_scatter(item_term(jnp.int32(0), lax.axis_size('sub') * shard_row...]
    pallas_call x0 -> x1, Pallas kernels: none -> 62.8 us  [on_device(): pl.pallas_call(functools.partial(kernel, n_grp, n_sub, ticks, parts), out...]
    all_gather x4 -> x0, blocking collectives: 57.5 us -> none  [on_device(): item_block = lax.all_gather(item_shard, 'sub', axis=0, tiled=True)]
    dot_general x12 -> x0, matrix products: 20.4 us -> none  [the longest x4 10.1 us: item_term(): jnp.dot(errors.T, current_users, precision=lax.Precision.HIGHEST, preferr...]
    ppermute x4 -> x0, waiting for transfers between devices: 13.3 us -> none  [passed_along(): return lax.ppermute(value, axis, pairs)]
    slice x1 -> x0, local copies, waits for them, and re-layouts: 8.88 us -> none  [on_device(): ratings[:, tick_index, :]]
    unnamed x11 -> x8, local copies, waits for them, and re-layouts: 0.65 us -> 4.36 us
    add x4 -> x0, other arithmetic: 3.41 us -> none  [on_device(): item_shard = item_shard + item_rate * (summed - shrink_rate * item_shard)]
  transfers between devices with their start and end apart: 8 -> 0, of which waited for: 8 -> 0; matrix products, arithmetic and copies ran while one was open for 3% -> 0% of each run, Pallas kernels for 0% -> 0%
where the time goes in v1:
time: 68.1 us; the launch traced here: 67.9 us
  Pallas kernels  62.8 us (92%)
  local copies, waits for them, and re-layouts  4.46 us (7%)
    pallas_call x1, Pallas kernels, on_device(): pl.pallas_call(functools.partial(kernel, n_grp, n_sub, ticks, parts), out...  62.8 us
    unnamed x8, local copies, waits for them, and re-layouts  4.36 us

profile of v1, /device:TPU:0, one launch (start us, length us, event | category | flops | bytes accessed | tf_op | source)
XLA Modules:
  0.0 67.9 jit_solution(14971397902740852633)
XLA Ops:
  0.6 0.8 %copy.8 = s32[8,4,2]{2,1,0:T(4,128)S(1)} copy(s32[8,4,2]{0,2,1:T(2,128)} %param.5) | data formatting | bytes 512 | tf_op args[1]
  1.4 0.1 reshape.7.marks
  1.5 0.0 copy-start
  1.5 0.0 copy-start.1
  1.6 2.0 %copy.11 = bf16[1024,4,256]{2,0,1:T(8,128)(2,1)S(1)} copy(bf16[1024,4,256]{2,1,0:T(4,128)(2,1)} %param.4) | data formatting | bytes 4194304 | tf_op args[0]
  3.5 0.0 copy-done
  3.5 0.0 copy-done.1
  3.5 62.8 %shard_map.59 = (f32[1024,256]{1,0:T(8,128)S(1)}, f32[64,256]{1,0:T(8,128)S(1)}) custom-call(s32[64]{0:T(128)S(1)} %reshape.7.marks, bf16[4,1024,256]{2,1,0:T(8,128)(2,1)S(1)} %bitcast.3, f32[1024,256]{1,0:T(8,128)S(1)} %copy-done, f32[64,256]{1,0:T(8,128)S(1)} %copy-done.1), custom_call_target="tpu_custom_call" | custom-call | tf_op jit(solution)/shard_map/pallas_call | solution.py:181
  66.3 1.0 %copy.14 = f32[1024,256]{1,0:T(8,128)} copy(f32[1024,256]{1,0:T(8,128)S(1)} %get-tuple-element.4) | data formatting | bytes 2097152
  67.3 0.6 copy.15
Async XLA Ops:
  1.5 2.0 %copy-start = (f32[1024,256]{1,0:T(8,128)S(1)}, f32[1024,256]{1,0:T(8,128)}, u32[]{:S(2)}) copy-start(f32[1024,256]{1,0:T(8,128)} %users.1) | copy-start | bytes 3145732
  1.5 2.0 %copy-start.1 = (f32[64,256]{1,0:T(8,128)S(1)}, f32[64,256]{1,0:T(8,128)}, u32[]{:S(2)}) copy-start(f32[64,256]{1,0:T(8,128)} %items.1) | copy-start | bytes 196612

commit v2 on v1

--- a/solution.py
+++ b/solution.py
@@ -40,7 +40,10 @@
     after = lax.rem(grp + 1, n_grp)
     before = lax.rem(grp + n_grp - 1, n_grp)
     shard = items.shape[0]
-    piece = TILE // n_sub
+    width = vbuf.shape[1] // parts
+    piece = width // n_sub
+    items_wide = vbuf.shape[1] // TILE
+    span = min(TILE, width)
     user_tiles = users.shape[0] // TILE
 
     barrier = pltpu.get_barrier_semaphore()
@@ -50,12 +53,14 @@
         pl.semaphore_signal(barrier, inc=1, device_id=(before, lax.rem(sub + k, n_sub)), device_id_type=MESH)
     pl.semaphore_wait(barrier, 2 * n_sub - 1)
 
+    order = sorted(range(1, n_sub), key=lambda k: (-min(k, n_sub - k), -k))
+
     def init_copy(k):
         peer = lax.rem(sub + k, n_sub)
         return pltpu.make_async_remote_copy(
             src_ref=items,
             dst_ref=vbuf.at[0, pl.ds(sub * shard, shard), :],
-            send_sem=init_send.at[k], recv_sem=init_recv.at[k],
+            send_sem=init_send.at[k], recv_sem=init_recv.at[sub],
             device_id=(grp, peer), device_id_type=MESH,
         )
 
@@ -66,8 +71,6 @@
     uh[...] = high
     ul[...] = low
     users_out[...] = users[...]
-    for k in range(1, n_sub):
-        init_copy(k).wait()
 
     def rs_copy(t, p, k):
         peer = lax.rem(sub + k, n_sub)
@@ -82,13 +85,13 @@
         peer = lax.rem(sub + k, n_sub)
         return pltpu.make_async_remote_copy(
             src_ref=stage.at[p],
-            dst_ref=vbuf.at[t + 1, pl.ds(p * TILE + sub * piece, piece), :],
+            dst_ref=vbuf.at[t + 1, pl.ds(p * width + sub * piece, piece), :],
             send_sem=ag_send.at[p, k], recv_sem=ag_recv.at[t, p, k],
             device_id=(after, peer), device_id_type=MESH,
         )
 
     def fin_copy(p):
-        row = p * TILE + sub * piece
+        row = p * width + sub * piece
         return pltpu.make_async_remote_copy(
             src_ref=stage.at[p],
             dst_ref=vfin.at[pl.ds(lax.rem(row, shard), piece), :],
@@ -98,26 +101,44 @@
 
     def tick(t, carry):
         for p in range(parts):
-            cols = slice(p * TILE, (p + 1) * TILE)
+            cols = slice(p * width, (p + 1) * width)
 
             @pl.when(t > 0)
             def _():
                 for k in range(n_sub):
                     ag_copy(t - 1, p, k).wait_recv()
+
+            for source in range(p * width // shard, (p + 1) * width // shard):
+                @pl.when(jnp.logical_and(t == 0, source != sub))
+                def _():
+                    pltpu.make_async_remote_copy(
+                        src_ref=items, dst_ref=vbuf.at[0, pl.ds(source * shard, shard), :],
+                        send_sem=init_send.at[0], recv_sem=init_recv.at[source],
+                        device_id=(grp, source), device_id_type=MESH,
+                    ).wait_recv()
 
             vh, vl = split(vbuf[t, cols, :])
             pred = mm(uh[...], vh, NT) + mm(uh[...], vl, NT) + mm(ul[...], vh, NT)
             for i in range(user_tiles):
                 rows = slice(i * TILE, (i + 1) * TILE)
-                mark = marks[(i * ticks + t) * parts + p].astype(jnp.float32)
-                error = mark * (ratings[t, rows, cols].astype(jnp.float32) - pred[rows, :])
-                high, low = split(error)
-                eh[rows, cols] = high
-                el[rows, cols] = low
+                for start in range(p * width, (p + 1) * width, span):
+                    some = slice(start, start + span)
+                    mark = marks[(i * ticks + t) * items_wide + start // TILE].astype(jnp.float32)
+                    guess = pred[rows, start - p * width : start - p * width + span]
+                    error = mark * (ratings[t, rows, some].astype(jnp.float32) - guess)
+                    high, low = split(error)
+                    eh[rows, some] = high
+                    el[rows, some] = low
+
+            @pl.when(t > 0)
+            def _():
+                for k in range(1, n_sub):
+                    rs_copy(t - 1, p, k).wait_send()
+
             gbuf[p] = (
                 mm(eh[:, cols], uh[...], TN) + mm(eh[:, cols], ul[...], TN) + mm(el[:, cols], uh[...], TN)
             )
-            for k in range(1, n_sub):
+            for k in order:
                 rs_copy(t, p, k).start()
 
         vh, vl = split(vbuf[t])
@@ -134,31 +155,32 @@
             for k in range(1, n_sub):
                 rs_copy(t, p, k).wait_recv()
                 total = total + rbuf[t, p, k]
-            mine = vbuf[t, pl.ds(p * TILE + sub * piece, piece), :]
+            mine = vbuf[t, pl.ds(p * width + sub * piece, piece), :]
+
+            @pl.when(t > 0)
+            def _():
+                for k in range(n_sub):
+                    ag_copy(t - 1, p, k).wait_send()
+
             stage[p] = mine + item_rate * (total - shrink_rate * mine)
 
             @pl.when(t < ticks - 1)
             def _():
-                for k in range(n_sub):
+                for k in [0] + order:
                     ag_copy(t, p, k).start()
 
             @pl.when(t == ticks - 1)
             def _():
                 fin_copy(p).start()
 
-        for p in range(parts):
-            for k in range(1, n_sub):
-                rs_copy(t, p, k).wait_send()
-
-            @pl.when(t < ticks - 1)
-            def _():
-                for k in range(n_sub):
-                    ag_copy(t, p, k).wait_send()
-
         return carry
 
     lax.fori_loop(0, ticks, tick, 0)
+    for k in range(1, n_sub):
+        init_copy(k).wait_send()
     for p in range(parts):
+        for k in range(1, n_sub):
+            rs_copy(ticks - 1, p, k).wait_send()
         fin_copy(p).wait_send()
     for p in range(parts):
         pltpu.make_async_remote_copy(
@@ -173,7 +195,7 @@
     n_users, ticks, block = ratings.shape
     rank = user_factors.shape[1]
     parts = block // TILE
-    piece = TILE // n_sub
+    piece = block // parts // n_sub
     shard = item_factors.shape[0]
     f32, bf16 = jnp.float32, jnp.bfloat16
     dma = pltpu.SemaphoreType.DMA
@@ -192,7 +214,7 @@
             pltpu.VMEM((n_users, block), bf16),
             pltpu.VMEM((n_users, block), bf16),
             pltpu.VMEM((ticks, block, rank), f32),
-            pltpu.VMEM((parts, TILE, rank), f32),
+            pltpu.VMEM((parts, block // parts, rank), f32),
             pltpu.VMEM((ticks, parts, n_sub, piece, rank), f32),
             pltpu.VMEM((parts, piece, rank), f32),
             pltpu.VMEM((shard, rank), f32),

time: 68.1 us -> 66.2 us (0.972)
  Pallas kernels: 62.8 us -> 60.8 us
    pallas_call x1, Pallas kernels: 62.8 us -> 60.8 us  [on_device(): pl.pallas_call(functools.partial(kernel, n_grp, n_sub, ticks, parts), out...]
where the time goes in v2:
time: 66.2 us; the launch traced here: 66 us
  Pallas kernels  60.8 us (92%)
  local copies, waits for them, and re-layouts  4.46 us (7%)
  between operations  0.68 us (1%)
    pallas_call x1, Pallas kernels, on_device(): pl.pallas_call(functools.partial(kernel, n_grp, n_sub, ticks, parts), out...  60.8 us
    unnamed x8, local copies, waits for them, and re-layouts  4.36 us

profile of v2, /device:TPU:0, one launch (start us, length us, event | category | flops | bytes accessed | tf_op | source)
XLA Modules:
  0.0 66.0 jit_solution(2519952051188563631)
XLA Ops:
  0.6 0.8 %copy.8 = s32[8,4,2]{2,1,0:T(4,128)S(1)} copy(s32[8,4,2]{0,2,1:T(2,128)} %param.5) | data formatting | bytes 512 | tf_op args[1]
  1.4 0.1 reshape.7.marks
  1.5 0.0 copy-start
  1.5 0.0 copy-start.1
  1.6 2.0 %copy.11 = bf16[1024,4,256]{2,0,1:T(8,128)(2,1)S(1)} copy(bf16[1024,4,256]{2,1,0:T(4,128)(2,1)} %param.4) | data formatting | bytes 4194304 | tf_op args[0]
  3.5 0.0 copy-done
  3.5 0.0 copy-done.1
  3.5 60.8 %shard_map.59 = (f32[1024,256]{1,0:T(8,128)S(1)}, f32[64,256]{1,0:T(8,128)S(1)}) custom-call(s32[64]{0:T(128)S(1)} %reshape.7.marks, bf16[4,1024,256]{2,1,0:T(8,128)(2,1)S(1)} %bitcast.3, f32[1024,256]{1,0:T(8,128)S(1)} %copy-done, f32[64,256]{1,0:T(8,128)S(1)} %copy-done.1), custom_call_target="tpu_custom_call" | custom-call | tf_op jit(solution)/shard_map/pallas_call | solution.py:203
  64.4 1.0 %copy.14 = f32[1024,256]{1,0:T(8,128)} copy(f32[1024,256]{1,0:T(8,128)S(1)} %get-tuple-element.4) | data formatting | bytes 2097152
  65.3 0.6 copy.15
Async XLA Ops:
  1.5 2.0 %copy-start = (f32[1024,256]{1,0:T(8,128)S(1)}, f32[1024,256]{1,0:T(8,128)}, u32[]{:S(2)}) copy-start(f32[1024,256]{1,0:T(8,128)} %users.1) | copy-start | bytes 3145732
  1.5 2.0 %copy-start.1 = (f32[64,256]{1,0:T(8,128)S(1)}, f32[64,256]{1,0:T(8,128)}, u32[]{:S(2)}) copy-start(f32[64,256]{1,0:T(8,128)} %items.1) | copy-start | bytes 196612

commit v3 on v2

--- a/solution.py
+++ b/solution.py
@@ -51,6 +51,10 @@
         pl.semaphore_signal(barrier, inc=1, device_id=(grp, lax.rem(sub + k, n_sub)), device_id_type=MESH)
     for k in range(n_sub):
         pl.semaphore_signal(barrier, inc=1, device_id=(before, lax.rem(sub + k, n_sub)), device_id_type=MESH)
+    high, low = split(users[...])
+    uh[...] = high
+    ul[...] = low
+    users_out[...] = users[...]
     pl.semaphore_wait(barrier, 2 * n_sub - 1)
 
     order = sorted(range(1, n_sub), key=lambda k: (-min(k, n_sub - k), -k))
@@ -67,10 +71,6 @@
     for k in range(1, n_sub):
         init_copy(k).start()
     vbuf[0, pl.ds(sub * shard, shard), :] = items[...]
-    high, low = split(users[...])
-    uh[...] = high
-    ul[...] = low
-    users_out[...] = users[...]
 
     def rs_copy(t, p, k):
         peer = lax.rem(sub + k, n_sub)

time: 66.2 us -> 66.2 us (level)
  no operation moved by 1% of the time
where the time goes in v3:
time: 66.2 us; the launch traced here: 66 us
  Pallas kernels  60.8 us (92%)
  local copies, waits for them, and re-layouts  4.46 us (7%)
  between operations  0.68 us (1%)
    pallas_call x1, Pallas kernels, on_device(): pl.pallas_call(functools.partial(kernel, n_grp, n_sub, ticks, parts), out...  60.8 us
    unnamed x8, local copies, waits for them, and re-layouts  4.36 us

profile of v3, /device:TPU:0, one launch (start us, length us, event | category | flops | bytes accessed | tf_op | source)
XLA Modules:
  0.0 66.0 jit_solution(16684304320950227438)
XLA Ops:
  0.6 0.8 %copy.8 = s32[8,4,2]{2,1,0:T(4,128)S(1)} copy(s32[8,4,2]{0,2,1:T(2,128)} %param.5) | data formatting | bytes 512 | tf_op args[1]
  1.4 0.1 reshape.7.marks
  1.5 0.0 copy-start
  1.5 0.0 copy-start.1
  1.6 2.0 %copy.11 = bf16[1024,4,256]{2,0,1:T(8,128)(2,1)S(1)} copy(bf16[1024,4,256]{2,1,0:T(4,128)(2,1)} %param.4) | data formatting | bytes 4194304 | tf_op args[0]
  3.5 0.0 copy-done
  3.5 0.0 copy-done.1
  3.5 60.8 %shard_map.59 = (f32[1024,256]{1,0:T(8,128)S(1)}, f32[64,256]{1,0:T(8,128)S(1)}) custom-call(s32[64]{0:T(128)S(1)} %reshape.7.marks, bf16[4,1024,256]{2,1,0:T(8,128)(2,1)S(1)} %bitcast.3, f32[1024,256]{1,0:T(8,128)S(1)} %copy-done, f32[64,256]{1,0:T(8,128)S(1)} %copy-done.1), custom_call_target="tpu_custom_call" | custom-call | tf_op jit(solution)/shard_map/pallas_call | solution.py:203
  64.4 1.0 %copy.14 = f32[1024,256]{1,0:T(8,128)} copy(f32[1024,256]{1,0:T(8,128)S(1)} %get-tuple-element.4) | data formatting | bytes 2097152
  65.3 0.6 copy.15
Async XLA Ops:
  1.5 2.0 %copy-start = (f32[1024,256]{1,0:T(8,128)S(1)}, f32[1024,256]{1,0:T(8,128)}, u32[]{:S(2)}) copy-start(f32[1024,256]{1,0:T(8,128)} %users.1) | copy-start | bytes 3145732
  1.5 2.0 %copy-start.1 = (f32[64,256]{1,0:T(8,128)S(1)}, f32[64,256]{1,0:T(8,128)}, u32[]{:S(2)}) copy-start(f32[64,256]{1,0:T(8,128)} %items.1) | copy-start | bytes 196612
